TPU v7x, 32 devices: a whole 2x2x4 slice. The times are simulated.
32 devices in a mesh: grp: 2 (over x), ch: 16 (over z, y, core).
Axes of the slice: x: 2, y: 2, z: 4, core: 2. Of those that a mesh axis runs over, the one named last changes fastest.
Arguments:
- features: bfloat16 [2048, 2048], P('ch', 'grp'), parts along dimension 1, may hold values from -50 to 50
- dw_weight: float32 [2048, 49], P('ch'), may hold values from -0.875 to 0.875
- norm_gain: float32 [2048], replicated, may hold values from 0.25 to 1.75
- layer_scale: float32 [2048], replicated, may hold values from 0.2 to 1
- w_in: bfloat16 [8192, 2048], P('ch'), may hold values from -0.125 to 0.125
- w_out: bfloat16 [8192, 2048], P('ch'), may hold values from -0.0625 to 0.0625
- w_head: bfloat16 [2048, 150], replicated, may hold values from -3 to 3
- labels: int32 [2048], P('grp'), parts along dimension 0, may hold values from 0 to 149
Outputs:
- d_features: float32 [2048, 2048], P('ch', 'grp'), parts along dimension 1
- d_dw: float32 [2048, 98], P('ch', 'grp'), parts along dimension 1
- d_scale: float32 [4096], P(('grp', 'ch')), parts along dimension 0
- d_w_in: float32 [16384, 2048], P(('grp', 'ch')), parts along dimension 0
- d_w_out: float32 [16384, 2048], P(('grp', 'ch')), parts along dimension 0
- d_head: float32 [2048, 300], P('ch', 'grp'), parts along dimension 1
- mean_loss: float32 [2], P('grp'), parts along dimension 0
There are 2 independent parts, one for each index of `grp`. A program takes and returns all parts, laid end to end along the dimension named above; an argument that names none is the same for every part. Nothing has to cross between parts.
All inputs are finite; a program needn't handle non-finite values.
Results may differ from a plain program's by a relative error of at most 0.012.
Values may be sent and summed in bfloat16 or wider, within the bound.
A program may use at most 128 MiB of HBM per device.

v0:
```python
import jax
import jax.numpy as jnp
from jax import lax
from jax.sharding import PartitionSpec as P

KS = 7
WIN_H = 32
WIN_W = 32
norm_eps = 1e-06


def conv_apply(in_grid, kernel):
    half = KS // 2
    padded = jnp.pad(in_grid, ((0, 0), (half, half), (half, half)))
    running = jnp.zeros(in_grid.shape, in_grid.dtype)
    for row_shift in range(KS):
        for col_shift in range(KS):
            tap = kernel[:, row_shift * KS + col_shift]
            running = (
                running
                + tap[:, None, None]
                * padded[:, row_shift : row_shift + WIN_H, col_shift : col_shift + WIN_W]
            )
    return running


def gelu_parts(values):
    cum_prob = 0.5 * (1.0 + lax.erf(values * 0.7071067811865476))
    density = jnp.exp(-0.5 * values * values) * 0.3989422804014327
    return (values * cum_prob, cum_prob + values * density)


def per_device(features, dw_weight, norm_gain, layer_scale, w_in, w_out, w_head, labels):
    highest = lax.Precision.HIGHEST
    my_rows = features.shape[0]
    tok_count = features.shape[1]
    class_count = w_head.shape[1]
    row_offset = lax.axis_index("ch") * my_rows
    inputs_wide = features.astype(jnp.float32)
    in_grid = inputs_wide.reshape(my_rows, WIN_H, WIN_W)
    conv_out = conv_apply(in_grid, dw_weight).reshape(my_rows, tok_count).astype(jnp.bfloat16)
    conv_all = lax.all_gather(conv_out, "ch", axis=0, tiled=True)
    conv_wide = conv_all.astype(jnp.float32)
    tok_mean = jnp.mean(conv_wide, axis=0)
    centered = conv_wide - tok_mean[None, :]
    tok_var = jnp.mean(centered * centered, axis=0)
    inv_std = 1.0 / jnp.sqrt(tok_var + norm_eps)
    normed = centered * inv_std[None, :]
    norm_out = (norm_gain[:, None] * normed).astype(jnp.bfloat16)
    pre_act = jnp.dot(w_in, norm_out, preferred_element_type=jnp.float32)
    gelu_out, gelu_slope = gelu_parts(pre_act)
    hidden = gelu_out.astype(jnp.bfloat16)
    my_scale = lax.dynamic_slice_in_dim(layer_scale, row_offset, my_rows, 0)
    head_wide = w_head.astype(jnp.float32)
    my_head = lax.dynamic_slice_in_dim(head_wide, row_offset, my_rows, 0)
    w_cols = w_out
    branch_sum = lax.psum_scatter(
        lax.dot_general(
            w_cols, hidden, (((0,), (0,)), ((), ())), preferred_element_type=jnp.float32
        ),
        "ch",
        scatter_dimension=0,
        tiled=True,
    )
    block_out = inputs_wide + my_scale[:, None] * branch_sum
    part_logits = lax.dot_general(block_out, my_head, (((0,), (0,)), ((), ())), precision=highest)
    logits = lax.psum(part_logits, "ch")
    row_max = jnp.max(logits, axis=1, keepdims=True)
    exp_terms = jnp.exp(logits - row_max)
    exp_total = jnp.sum(exp_terms, axis=1, keepdims=True)
    log_total = jnp.log(exp_total) + row_max
    onehot = (labels[:, None] == jnp.arange(class_count, dtype=jnp.int32)[None, :]).astype(
        jnp.float32
    )
    picked = jnp.sum(logits * onehot, axis=1)
    mean_loss = jnp.mean(log_total[:, 0] - picked).reshape(1)
    logit_grad = exp_terms / exp_total - onehot
    out_grad = lax.dot_general(my_head, logit_grad, (((1,), (1,)), ((), ())), precision=highest)
    d_head = jnp.dot(block_out, logit_grad, precision=highest)
    d_scale = jnp.sum(out_grad * branch_sum, axis=1)
    branch_grad = (my_scale[:, None] * out_grad).astype(jnp.bfloat16)
    incoming = lax.all_gather(branch_grad, "ch", axis=0, tiled=True)
    w_cols = w_out
    hidden_acc = jnp.dot(w_cols, incoming, preferred_element_type=jnp.float32)
    tile_grad = lax.dot_general(
        hidden, incoming, (((1,), (1,)), ((), ())), preferred_element_type=jnp.float32
    )
    pre_grad = (hidden_acc * gelu_slope).astype(jnp.bfloat16)
    d_w_in = lax.dot_general(
        pre_grad, norm_out, (((1,), (1,)), ((), ())), preferred_element_type=jnp.float32
    )
    norm_grad = lax.dot_general(
        w_in, pre_grad, (((0,), (0,)), ((), ())), preferred_element_type=jnp.float32
    )
    gained = norm_gain[:, None] * norm_grad
    conv_term = (
        gained
        - jnp.mean(gained, axis=0)[None, :]
        - normed * jnp.mean(gained * normed, axis=0)[None, :]
    ) * inv_std[None, :]
    conv_grad = lax.psum_scatter(conv_term, "ch", scatter_dimension=0, tiled=True)
    unused, pullback = jax.vjp(conv_apply, in_grid, dw_weight)
    grid_grad, d_dw = pullback(conv_grad.reshape(my_rows, WIN_H, WIN_W))
    d_features = out_grad + grid_grad.reshape(my_rows, tok_count)
    return (d_features, d_dw, d_scale, d_w_in, tile_grad, d_head, mean_loss)


def solution(mesh):
    placed = (P("ch", "grp"), P("ch", None), P(), P(), P("ch", None), P("ch", None), P(), P("grp"))
    return jax.shard_map(
        per_device,
        mesh=mesh,
        in_specs=placed,
        out_specs=(
            P("ch", "grp"),
            P("ch", "grp"),
            P(("grp", "ch")),
            P(("grp", "ch"), None),
            P(("grp", "ch"), None),
            P("ch", "grp"),
            P("grp"),
        ),
        check_vma=False,
    )
```

profile of v0, /device:TPU:0, one launch (start us, length us, event | category | flops | bytes accessed | tf_op | source)
XLA Modules:
  0.0 497.7 jit_solution(14007070145774544614)
XLA Ops:
  10.4 1.1 copy.19
  11.6 4.8 add_convert_fusion
  16.5 56.0 %all-gather.3.cloned.1.call-done = bf16[2048,1024]{0,1:T(8,128)(2,1)} async-done(((bf16[128,1024]{0,1:T(8,128)(2,1)}), bf16[2048,1024]{0,1:T(8,128)(2,1)}) %all-gather.3.cloned.1.call-update) | async-done | bytes 4194320 | tf_op jit(solution)/shard_map/all_gather | solution.py:42
  72.5 3.0 convert_reduce_fusion
  75.9 1.2 fusion.9
  77.3 1.6 fusion.5
  79.0 2.4 fusion.31
  81.4 1.3 copy-done.7
  82.7 5.6 %convolution_bitcast_fusion = f32[2048,1024]{0,1:T(8,128)} fusion(bf16[512,2048]{1,0:T(8,128)(2,1)S(1)} %copy-done.45, f32[1024,512]{1,0:T(8,128)S(1)} %fusion.31), kind=kOutput, calls=%fused_computation.62 | convolution fusion | flops 2150105088 | bytes 12582912 | tf_op jit(solution)/shard_map/dot_general | solution.py:58
  89.2 102.4 %reduce-scatter.3.cloned.1.call-done = f32[128,1024]{0,1:T(8,128)} async-done(((f32[2048,1024]{0,1:T(8,128)}), f32[128,1024]{0,1:T(8,128)}) %reduce-scatter.3.cloned.1.call-update) | async-done | bytes 524304 | tf_op jit(solution)/shard_map/reduce_scatter | solution.py:57
  191.5 2.6 fusion.22
  194.2 91.7 %all-reduce.101.cloned.1.call-done = f32[1024,150]{0,1:T(8,128)} async-done(((f32[1024,150]{0,1:T(8,128)}), f32[1024,150]{0,1:T(8,128)}) %all-reduce.101.cloned.1.call-update) | async-done | bytes 614416 | tf_op jit(solution)/shard_map/psum | solution.py:67
  285.9 1.1 reduce_max.9
  287.0 1.2 select_reduce_fusion
  288.2 1.7 fusion.23
  290.9 2.5 multiply_reduce_fusion.1
  293.7 53.5 %all-gather.5.cloned.1.call-done = bf16[2048,1024]{0,1:T(8,128)(2,1)} async-done(((bf16[128,1024]{0,1:T(8,128)(2,1)}), bf16[2048,1024]{0,1:T(8,128)(2,1)}) %all-gather.5.cloned.1.call-update) | async-done | bytes 4194320 | tf_op jit(solution)/shard_map/all_gather | solution.py:82
  347.2 6.5 %fusion.15 = bf16[512,1024]{0,1:T(8,128)(2,1)S(1)} fusion(f32[1024,512]{1,0:T(8,128)} %copy-done.7, bf16[2048,1024]{0,1:T(8,128)(2,1)} %all-gather.5.cloned.1.call-done, bf16[512,2048]{1,0:T(8,128)(2,1)} %param.13), kind=kOutput, calls=%fused_computation.69 | convolution fusion | flops 2152726528 | bytes 9437184 | tf_op jit(solution)/shard_map/dot_general | solution.py:84
  353.7 3.0 fusion.6
  357.3 5.4 %fusion.8 = f32[2048,1024]{0,1:T(8,128)} fusion(bf16[2048,1024]{0,1:T(8,128)(2,1)S(1)} %copy-done.3, f32[1024,2048]{1,0:T(8,128)S(1)} %get-tuple-element.158, f32[1024]{0:T(1024)S(1)} %get-tuple-element.159, f32[1024]{0:T(1024)S(1)} %get-tuple-element.160, f32[2048]{0:T(1024)S(1)} %copy-done.13, f32[1024]{0:T(1024)S(1)} %add_rsqrt_fusion, ...), kind=kLoop, calls=%fused_computation.10 | loop fusion | flops 16777216 | bytes 20996096 | tf_op jit(solution)/shard_map/mul | solution.py:96
  364.1 1.5 fusion.21
  365.6 7.4 %fusion.32 = f32[512,2048]{1,0:T(8,128)} fusion(bf16[512,1024]{0,1:T(8,128)(2,1)} %copy-done.10, bf16[2048,1024]{0,1:T(8,128)(2,1)} %copy-done.4), kind=kOutput, calls=%fused_computation.255 | convolution fusion | flops 2147483648 | bytes 9437184 | tf_op jit(solution)/shard_map/dot_general | solution.py:89
  372.9 4.5 fusion.28
  377.5 88.5 %reduce-scatter.5.cloned.1.call-done = f32[128,1024]{0,1:T(8,128)} async-done(((f32[2048,1024]{0,1:T(8,128)}), f32[128,1024]{0,1:T(8,128)}) %reduce-scatter.5.cloned.1.call-update) | async-done | bytes 524304 | tf_op jit(solution)/shard_map/reduce_scatter | solution.py:101
  465.9 2.9 broadcast_multiply_fusion.2
  470.0 2.4 broadcast_multiply_fusion
  472.4 6.0 %pad_add_fusion = f32[128,38,38]{0,2,1:T(8,128)S(1)} fusion(f32[128,32,32]{0,2,1:T(8,128)S(1)} %get-tuple-element.66, f32[128,32,32]{0,2,1:T(8,128)S(1)} %get-tuple-element.67, f32[128,32,32]{0,2,1:T(8,128)S(1)} %get-tuple-element.68, f32[128,32,32]{0,2,1:T(8,128)S(1)} %get-tuple-element.69, f32[128,32,32]{0,2,1:T(8,128)S(1)} %get-tuple-element.70, ...), kind=kLoop, calls=%fused_computation.76 | loop fusion | flops 7762944 | bytes 23283712 | tf_op jit(solution)/shard_map/transpose(jvp())/add_any | solution.py:22
  478.4 3.1 pad_add_fusion.1
  481.5 2.1 copy.21
  483.5 2.1 add.438
  486.4 1.4 multiply_reduce_fusion.49
  487.8 1.4 multiply_reduce_fusion.50
  (116 shorter events, 9.8 us)
Async XLA Ops:
  7.2 71.8 %copy-start = (bf16[512,2048]{1,0:T(8,128)(2,1)S(1)}, bf16[512,2048]{1,0:T(8,128)(2,1)}, u32[]{:S(2)}) copy-start(bf16[512,2048]{1,0:T(8,128)(2,1)} %param.12) | copy-start | bytes 6291460
  7.2 65.3 %all-gather.3.cloned.1.call-start = ((), (), s32[]{:S(2)}) async-start(), calls=%async_computation.2 | async-start | bytes 4456448 | tf_op jit(solution)/shard_map/all_gather | solution.py:42
  9.2 67.9 %copy-start.29 = (f32[128]{0:T(128)}, f32[128]{0:T(128)S(1)}, u32[]{:S(2)}) copy-start(f32[128]{0:T(128)S(1)} %get-tuple-element.110) | copy-start | bytes 1540
  9.2 67.9 %copy-start.30 = (f32[128]{0:T(128)}, f32[128]{0:T(128)S(1)}, u32[]{:S(2)}) copy-start(f32[128]{0:T(128)S(1)} %get-tuple-element.111) | copy-start | bytes 1540
  9.2 67.9 %copy-start.31 = (f32[128]{0:T(128)}, f32[128]{0:T(128)S(1)}, u32[]{:S(2)}) copy-start(f32[128]{0:T(128)S(1)} %get-tuple-element.112) | copy-start | bytes 1540
  9.2 67.9 %copy-start.32 = (f32[128]{0:T(128)}, f32[128]{0:T(128)S(1)}, u32[]{:S(2)}) copy-start(f32[128]{0:T(128)S(1)} %get-tuple-element.113) | copy-start | bytes 1540
  9.3 67.9 %copy-start.33 = (f32[128]{0:T(128)}, f32[128]{0:T(128)S(1)}, u32[]{:S(2)}) copy-start(f32[128]{0:T(128)S(1)} %get-tuple-element.114) | copy-start | bytes 1540
  9.3 67.9 %copy-start.34 = (f32[128]{0:T(128)}, f32[128]{0:T(128)S(1)}, u32[]{:S(2)}) copy-start(f32[128]{0:T(128)S(1)} %get-tuple-element.115) | copy-start | bytes 1540
  9.3 67.9 %copy-start.35 = (f32[128]{0:T(128)}, f32[128]{0:T(128)S(1)}, u32[]{:S(2)}) copy-start(f32[128]{0:T(128)S(1)} %get-tuple-element.116) | copy-start | bytes 1540
  9.3 67.9 %copy-start.36 = (f32[128]{0:T(128)}, f32[128]{0:T(128)S(1)}, u32[]{:S(2)}) copy-start(f32[128]{0:T(128)S(1)} %get-tuple-element.117) | copy-start | bytes 1540
  9.3 67.9 %copy-start.37 = (f32[128]{0:T(128)}, f32[128]{0:T(128)S(1)}, u32[]{:S(2)}) copy-start(f32[128]{0:T(128)S(1)} %get-tuple-element.118) | copy-start | bytes 1540
  9.3 67.9 %copy-start.38 = (f32[128]{0:T(128)}, f32[128]{0:T(128)S(1)}, u32[]{:S(2)}) copy-start(f32[128]{0:T(128)S(1)} %get-tuple-element.119) | copy-start | bytes 1540
  9.3 67.9 %copy-start.39 = (f32[128]{0:T(128)}, f32[128]{0:T(128)S(1)}, u32[]{:S(2)}) copy-start(f32[128]{0:T(128)S(1)} %get-tuple-element.120) | copy-start | bytes 1540
  9.3 67.9 %copy-start.40 = (f32[128]{0:T(128)}, f32[128]{0:T(128)S(1)}, u32[]{:S(2)}) copy-start(f32[128]{0:T(128)S(1)} %get-tuple-element.121) | copy-start | bytes 1540
  10.4 65.1 %copy-start.20 = (f32[128]{0:T(128)}, f32[128]{0:T(128)S(1)}, u32[]{:S(2)}) copy-start(f32[128]{0:T(128)S(1)} %get-tuple-element.136) | copy-start | bytes 1540
  10.4 65.1 %copy-start.22 = (f32[128]{0:T(128)}, f32[128]{0:T(128)S(1)}, u32[]{:S(2)}) copy-start(f32[128]{0:T(128)S(1)} %get-tuple-element.137) | copy-start | bytes 1540
  10.4 66.9 %copy-start.24 = (f32[128]{0:T(128)}, f32[128]{0:T(128)S(1)}, u32[]{:S(2)}) copy-start(f32[128]{0:T(128)S(1)} %get-tuple-element.138) | copy-start | bytes 1540
  10.4 66.9 %copy-start.26 = (f32[128]{0:T(128)}, f32[128]{0:T(128)S(1)}, u32[]{:S(2)}) copy-start(f32[128]{0:T(128)S(1)} %get-tuple-element.139) | copy-start | bytes 1540
  16.4 175.1 %reduce-scatter.3.cloned.1.call-start = ((), (), s32[]{:S(2)}) async-start(), calls=%async_computation.3 | async-start | bytes 8912896 | tf_op jit(solution)/shard_map/reduce_scatter | solution.py:57
  88.3 198.7 %copy-start.41 = (s32[1024]{0:T(1024)S(1)}, s32[1024]{0:T(1024)}, u32[]{:S(2)}) copy-start(s32[1024]{0:T(1024)} %param.15) | copy-start | bytes 12292
  88.4 197.5 %all-reduce.101.cloned.1.call-start = ((), (), s32[]{:S(2)}) async-start(), calls=%async_computation.4 | async-start | bytes 1245184 | tf_op jit(solution)/shard_map/psum | solution.py:67
  89.2 105.0 %copy-start.43 = (f32[128]{0:T(128)}, f32[128]{0:T(128)S(1)}, u32[]{:S(2)}) copy-start(f32[128]{0:T(128)S(1)} %dynamic_slice.7) | copy-start | bytes 1540
  194.1 153.1 %all-gather.5.cloned.1.call-start = ((), (), s32[]{:S(2)}) async-start(), calls=%async_computation.5 | async-start | bytes 4456448 | tf_op jit(solution)/shard_map/all_gather | solution.py:82
  289.9 63.7 %copy-start.11 = (f32[128,1024]{1,0:T(8,128)}, f32[128,1024]{1,0:T(8,128)S(1)}, u32[]{:S(2)}) copy-start(f32[128,1024]{1,0:T(8,128)S(1)} %fusion.23) | copy-start | bytes 1572868
  293.4 172.5 %reduce-scatter.5.cloned.1.call-start = ((), (), s32[]{:S(2)}) async-start(), calls=%async_computation.6 | async-start | bytes 8912896 | tf_op jit(solution)/shard_map/reduce_scatter | solution.py:101
  377.4 91.4 %copy-start.15 = (f32[128]{0:T(128)S(1)}, f32[128]{0:T(128)}, u32[]{:S(2)}) copy-start(f32[128]{0:T(128)} %copy-done.14) | copy-start | bytes 1540
  377.4 91.4 %copy-start.17 = (f32[128]{0:T(128)S(1)}, f32[128]{0:T(128)}, u32[]{:S(2)}) copy-start(f32[128]{0:T(128)} %copy-done.16) | copy-start | bytes 1540
  377.4 91.4 %copy-start.19 = (f32[128]{0:T(128)S(1)}, f32[128]{0:T(128)}, u32[]{:S(2)}) copy-start(f32[128]{0:T(128)} %copy-done.18) | copy-start | bytes 1540
  377.5 91.4 %copy-start.21 = (f32[128]{0:T(128)S(1)}, f32[128]{0:T(128)}, u32[]{:S(2)}) copy-start(f32[128]{0:T(128)} %copy-done.20) | copy-start | bytes 1540
  377.5 91.4 %copy-start.23 = (f32[128]{0:T(128)S(1)}, f32[128]{0:T(128)}, u32[]{:S(2)}) copy-start(f32[128]{0:T(128)} %copy-done.22) | copy-start | bytes 1540
  377.5 91.4 %copy-start.25 = (f32[128]{0:T(128)S(1)}, f32[128]{0:T(128)}, u32[]{:S(2)}) copy-start(f32[128]{0:T(128)} %copy-done.24) | copy-start | bytes 1540
  377.5 91.4 %copy-start.27 = (f32[128]{0:T(128)S(1)}, f32[128]{0:T(128)}, u32[]{:S(2)}) copy-start(f32[128]{0:T(128)} %copy-done.26) | copy-start | bytes 1540
  (19 other events, 197.3 us)
Sparse Core Ops, SparseCore 0:
  16.5 55.9 all-gather.2
  88.5 103.0 reduce-scatter.2
  195.5 90.2 all-reduce.100
  293.5 53.5 all-gather.4
  362.9 102.9 reduce-scatter.4
where the time goes:
time: 498 us
  waiting for transfers between devices  392 us (79%)
  other arithmetic  44 us (9%)
  matrix products  35 us (7%)
  between operations  16.2 us (3%)
  local copies, waits for them, and re-layouts  9.9 us (2%)
    reduce_scatter x1, waiting for transfers between devices, per_device(): lax.psum_scatter(lax.dot_general(w_cols, hidden, (((0,), (0,)), ((), ()))...  102 us
    psum x1, waiting for transfers between devices, per_device(): logits = lax.psum(part_logits, 'ch')  91.7 us
    reduce_scatter x1, waiting for transfers between devices, per_device(): lax.psum_scatter(conv_term, 'ch', scatter_dimension=0, tiled=True)  88.5 us
    all_gather x1, waiting for transfers between devices, per_device(): conv_all = lax.all_gather(conv_out, 'ch', axis=0, tiled=True)  56 us
    all_gather x1, waiting for transfers between devices, per_device(): incoming = lax.all_gather(branch_grad, 'ch', axis=0, tiled=True)  53.5 us
  transfers between devices with their start and end apart: 5, of which 5 were waited for; matrix products, arithmetic and copies ran while one was open for 3% of the time, Pallas kernels for 0%

commit v1 on v0

--- a/solution.py
+++ b/solution.py
@@ -7,6 +7,7 @@
 WIN_H = 32
 WIN_W = 32
 norm_eps = 1e-06
+trace_terms_on = lambda inputs: jnp.sum(lax.all_gather(inputs, "ch"), axis=0)
 
 
 def conv_apply(in_grid, kernel):
@@ -64,7 +65,7 @@
     )
     block_out = inputs_wide + my_scale[:, None] * branch_sum
     part_logits = lax.dot_general(block_out, my_head, (((0,), (0,)), ((), ())), precision=highest)
-    logits = lax.psum(part_logits, "ch")
+    logits = trace_terms_on(part_logits)
     row_max = jnp.max(logits, axis=1, keepdims=True)
     exp_terms = jnp.exp(logits - row_max)
     exp_total = jnp.sum(exp_terms, axis=1, keepdims=True)

time: 498 us -> 513 us (1.030); the launches traced: 498 us -> 505 us
  local copies, waits for them, and re-layouts: 9.9 us -> 23.6 us
  waiting for transfers between devices: 392 us -> 382 us
    psum x1 -> x0, waiting for transfers between devices: 91.7 us -> none  [per_device(): logits = lax.psum(part_logits, 'ch')]
    all_gather x0 -> x1, waiting for transfers between devices: none -> 84.4 us  [lax.all_gather(inputs, 'ch')]
    unnamed x93 -> x190, local copies, waits for them, and re-layouts: 3.12 us -> 15.2 us
where the time goes in v1:
time: 513 us; the launch traced here: 505 us
  waiting for transfers between devices  382 us (74%)
  other arithmetic  45.6 us (9%)
  matrix products  35.5 us (7%)
  local copies, waits for them, and re-layouts  23.6 us (5%)
  between operations  17.4 us (3%)
    reduce_scatter x1, waiting for transfers between devices, per_device(): lax.psum_scatter(lax.dot_general(w_cols, hidden, (((0,), (0,)), ((), ()))...  102 us
    reduce_scatter x1, waiting for transfers between devices, per_device(): lax.psum_scatter(conv_term, 'ch', scatter_dimension=0, tiled=True)  88.3 us
    all_gather x1, waiting for transfers between devices, lax.all_gather(inputs, 'ch')  84.4 us
    all_gather x1, waiting for transfers between devices, per_device(): conv_all = lax.all_gather(conv_out, 'ch', axis=0, tiled=True)  56 us
    all_gather x1, waiting for transfers between devices, per_device(): incoming = lax.all_gather(branch_grad, 'ch', axis=0, tiled=True)  51.3 us
    unnamed x190, local copies, waits for them, and re-layouts  15.2 us
  transfers between devices with their start and end apart: 5, of which 5 were waited for; matrix products, arithmetic and copies ran while one was open for 3% of the time, Pallas kernels for 0%

profile of v1, /device:TPU:0, one launch (start us, length us, event | category | flops | bytes accessed | tf_op | source)
XLA Modules:
  0.0 505.1 jit_solution(2474564495130163656)
XLA Ops:
  8.3 1.6 slice_bitcast_fusion.48
  12.4 5.4 %add_convert_fusion = bf16[128,32,32]{0,2,1:T(8,128)(2,1)} fusion(f32[128,32,32]{0,2,1:T(8,128)S(1)} %bitcast_convert_fusion, f32[128]{0:T(128)S(1)} %get-tuple-element.155, f32[128]{0:T(128)S(1)} %get-tuple-element.156, f32[128]{0:T(128)S(1)} %get-tuple-element.109, f32[128]{0:T(128)S(1)} %get-tuple-element.110, f32[128]{0:T(128)S(1)} %get-tuple-element.111, ...), kind=kLoop, calls=%fused_computation.141 | loop fusion | flops 12845056 | bytes 811520 | tf_op jit(solution)/shard_map/convert_element_type | solution.py:42
  17.8 56.0 %all-gather.5.cloned.1.call-done = bf16[2048,1024]{0,1:T(8,128)(2,1)} async-done(((bf16[128,1024]{0,1:T(8,128)(2,1)}), bf16[2048,1024]{0,1:T(8,128)(2,1)}) %all-gather.5.cloned.1.call-update) | async-done | bytes 4194320 | tf_op jit(solution)/shard_map/all_gather | solution.py:43
  73.8 3.0 convert_reduce_fusion
  78.9 1.6 fusion.5
  80.6 2.4 fusion.31
  83.0 1.3 copy-done.7
  84.3 5.6 %convolution_bitcast_fusion = f32[2048,1024]{0,1:T(8,128)} fusion(bf16[512,2048]{1,0:T(8,128)(2,1)S(1)} %copy-done.93, f32[1024,512]{1,0:T(8,128)S(1)} %fusion.31), kind=kOutput, calls=%fused_computation.63 | convolution fusion | flops 2150105088 | bytes 12582912 | tf_op jit(solution)/shard_map/dot_general | solution.py:59
  90.7 102.3 %reduce-scatter.3.cloned.1.call-done = f32[128,1024]{0,1:T(8,128)} async-done(((f32[2048,1024]{0,1:T(8,128)}), f32[128,1024]{0,1:T(8,128)}) %reduce-scatter.3.cloned.1.call-update) | async-done | bytes 524304 | tf_op jit(solution)/shard_map/reduce_scatter | solution.py:58
  193.1 2.6 fusion.22
  195.9 84.4 %all-gather.9.cloned.1.call-done = f32[16384,150]{0,1:T(8,128)} async-done(((f32[1024,150]{0,1:T(8,128)}), f32[16384,150]{0,1:T(8,128)}) %all-gather.9.cloned.1.call-update) | async-done | bytes 9830416 | tf_op jit(solution)/shard_map/all_gather | solution.py:10
  280.3 11.9 %copy.27 = f32[19,8,16,1024]{3,2,1,0:T(8,128)S(1)} copy(f32[19,8,16,1024]{3,1,2,0:T(8,128)} %bitcast.249) | data formatting | bytes 19922944
  292.2 2.3 bitcast_reduce_fusion
  295.4 2.2 fusion.23
  297.6 2.0 copy.24
  299.7 2.5 multiply_reduce_fusion.1
  302.4 51.3 %all-gather.7.cloned.1.call-done = bf16[2048,1024]{0,1:T(8,128)(2,1)} async-done(((bf16[128,1024]{0,1:T(8,128)(2,1)}), bf16[2048,1024]{0,1:T(8,128)(2,1)}) %all-gather.7.cloned.1.call-update) | async-done | bytes 4194320 | tf_op jit(solution)/shard_map/all_gather | solution.py:83
  353.7 6.5 %fusion.15 = bf16[512,1024]{0,1:T(8,128)(2,1)S(1)} fusion(f32[1024,512]{1,0:T(8,128)} %copy-done.7, bf16[2048,1024]{0,1:T(8,128)(2,1)} %all-gather.7.cloned.1.call-done, bf16[512,2048]{1,0:T(8,128)(2,1)} %param.13), kind=kOutput, calls=%fused_computation.70 | convolution fusion | flops 2152726528 | bytes 9437184 | tf_op jit(solution)/shard_map/dot_general | solution.py:85
  360.2 3.0 fusion.6
  363.9 5.4 %fusion.8 = f32[2048,1024]{0,1:T(8,128)} fusion(bf16[2048,1024]{0,1:T(8,128)(2,1)S(1)} %copy-done.3, f32[1024,2048]{1,0:T(8,128)S(1)} %get-tuple-element.158, f32[1024]{0:T(1024)S(1)} %get-tuple-element.159, f32[1024]{0:T(1024)S(1)} %get-tuple-element.160, f32[2048]{0:T(1024)S(1)} %copy-done.11, f32[1024]{0:T(1024)S(1)} %add_rsqrt_fusion, ...), kind=kLoop, calls=%fused_computation.11 | loop fusion | flops 16777216 | bytes 20996096 | tf_op jit(solution)/shard_map/mul | solution.py:97
  370.6 1.5 fusion.21
  372.0 7.4 %fusion.32 = f32[512,2048]{1,0:T(8,128)} fusion(bf16[512,1024]{0,1:T(8,128)(2,1)} %copy-done.9, bf16[2048,1024]{0,1:T(8,128)(2,1)} %copy-done.4), kind=kOutput, calls=%fused_computation.256 | convolution fusion | flops 2147483648 | bytes 9437184 | tf_op jit(solution)/shard_map/dot_general | solution.py:90
  379.5 4.5 fusion.28
  384.1 88.3 %reduce-scatter.5.cloned.1.call-done = f32[128,1024]{0,1:T(8,128)} async-done(((f32[2048,1024]{0,1:T(8,128)}), f32[128,1024]{0,1:T(8,128)}) %reduce-scatter.5.cloned.1.call-update) | async-done | bytes 524304 | tf_op jit(solution)/shard_map/reduce_scatter | solution.py:102
  472.5 3.0 broadcast_multiply_fusion.2
  477.0 2.4 broadcast_multiply_fusion
  479.4 6.1 %pad_add_fusion = f32[128,38,38]{0,2,1:T(8,128)S(1)} fusion(f32[128,32,32]{0,2,1:T(8,128)S(1)} %get-tuple-element.66, f32[128,32,32]{0,2,1:T(8,128)S(1)} %get-tuple-element.67, f32[128,32,32]{0,2,1:T(8,128)S(1)} %get-tuple-element.68, f32[128,32,32]{0,2,1:T(8,128)S(1)} %get-tuple-element.69, f32[128,32,32]{0,2,1:T(8,128)S(1)} %get-tuple-element.70, ...), kind=kLoop, calls=%fused_computation.77 | loop fusion | flops 7762944 | bytes 23283712 | tf_op jit(solution)/shard_map/transpose(jvp())/add_any | solution.py:23
  485.5 3.1 pad_add_fusion.1
  488.5 2.0 copy.25
  490.6 2.1 add.436
  493.4 1.4 multiply_reduce_fusion.49
  494.8 1.4 multiply_reduce_fusion.50
  (214 shorter events, 11.4 us)
Async XLA Ops:
  7.2 66.7 %all-gather.5.cloned.1.call-start = ((), (), s32[]{:S(2)}) async-start(), calls=%async_computation.2 | async-start | bytes 4456448 | tf_op jit(solution)/shard_map/all_gather | solution.py:43
  17.8 175.3 %reduce-scatter.3.cloned.1.call-start = ((), (), s32[]{:S(2)}) async-start(), calls=%async_computation.3 | async-start | bytes 8912896 | tf_op jit(solution)/shard_map/reduce_scatter | solution.py:58
  89.9 190.4 %all-gather.9.cloned.1.call-start = ((), (), s32[]{:S(2)}) async-start(), calls=%async_computation.6 | async-start | bytes 10584064 | tf_op jit(solution)/shard_map/all_gather | solution.py:10
  90.7 201.5 %copy-start.91 = (f32[128]{0:T(128)}, f32[128]{0:T(128)S(1)}, u32[]{:S(2)}) copy-start(f32[128]{0:T(128)S(1)} %dynamic_slice.7) | copy-start | bytes 1540
  195.6 158.1 %all-gather.7.cloned.1.call-start = ((), (), s32[]{:S(2)}) async-start(), calls=%async_computation.4 | async-start | bytes 4456448 | tf_op jit(solution)/shard_map/all_gather | solution.py:83
  302.2 170.2 %reduce-scatter.5.cloned.1.call-start = ((), (), s32[]{:S(2)}) async-start(), calls=%async_computation.5 | async-start | bytes 8912896 | tf_op jit(solution)/shard_map/reduce_scatter | solution.py:102
  379.4 93.0 %copy-start.75 = (f32[128]{0:T(128)S(1)}, f32[128]{0:T(128)}, u32[]{:S(2)}) copy-start(f32[128]{0:T(128)} %copy-done.74) | copy-start | bytes 1540
  379.4 93.0 %copy-start.77 = (f32[128]{0:T(128)S(1)}, f32[128]{0:T(128)}, u32[]{:S(2)}) copy-start(f32[128]{0:T(128)} %copy-done.76) | copy-start | bytes 1540
  379.4 93.0 %copy-start.79 = (f32[128]{0:T(128)S(1)}, f32[128]{0:T(128)}, u32[]{:S(2)}) copy-start(f32[128]{0:T(128)} %copy-done.78) | copy-start | bytes 1540
  379.4 93.0 %copy-start.81 = (f32[128]{0:T(128)S(1)}, f32[128]{0:T(128)}, u32[]{:S(2)}) copy-start(f32[128]{0:T(128)} %copy-done.80) | copy-start | bytes 1540
  379.4 93.0 %copy-start.83 = (f32[128]{0:T(128)S(1)}, f32[128]{0:T(128)}, u32[]{:S(2)}) copy-start(f32[128]{0:T(128)} %copy-done.82) | copy-start | bytes 1540
  379.4 93.0 %copy-start.85 = (f32[128]{0:T(128)S(1)}, f32[128]{0:T(128)}, u32[]{:S(2)}) copy-start(f32[128]{0:T(128)} %copy-done.84) | copy-start | bytes 1540
  379.5 93.0 %copy-start.87 = (f32[128]{0:T(128)S(1)}, f32[128]{0:T(128)}, u32[]{:S(2)}) copy-start(f32[128]{0:T(128)} %copy-done.86) | copy-start | bytes 1540
  379.5 93.0 %copy-start.89 = (f32[128]{0:T(128)S(1)}, f32[128]{0:T(128)}, u32[]{:S(2)}) copy-start(f32[128]{0:T(128)} %copy-done.88) | copy-start | bytes 1540
  384.0 91.5 %copy-start.39 = (f32[128]{0:T(128)S(1)}, f32[128]{0:T(128)}, u32[]{:S(2)}) copy-start(f32[128]{0:T(128)} %copy-done.38) | copy-start | bytes 1540
  384.0 91.5 %copy-start.41 = (f32[128]{0:T(128)S(1)}, f32[128]{0:T(128)}, u32[]{:S(2)}) copy-start(f32[128]{0:T(128)} %copy-done.40) | copy-start | bytes 1540
  384.0 91.5 %copy-start.43 = (f32[128]{0:T(128)S(1)}, f32[128]{0:T(128)}, u32[]{:S(2)}) copy-start(f32[128]{0:T(128)} %copy-done.42) | copy-start | bytes 1540
  384.0 91.5 %copy-start.45 = (f32[128]{0:T(128)S(1)}, f32[128]{0:T(128)}, u32[]{:S(2)}) copy-start(f32[128]{0:T(128)} %copy-done.44) | copy-start | bytes 1540
  384.0 91.5 %copy-start.47 = (f32[128]{0:T(128)S(1)}, f32[128]{0:T(128)}, u32[]{:S(2)}) copy-start(f32[128]{0:T(128)} %copy-done.46) | copy-start | bytes 1540
  384.0 91.5 %copy-start.49 = (f32[128]{0:T(128)S(1)}, f32[128]{0:T(128)}, u32[]{:S(2)}) copy-start(f32[128]{0:T(128)} %copy-done.48) | copy-start | bytes 1540
  384.0 91.5 %copy-start.51 = (f32[128]{0:T(128)S(1)}, f32[128]{0:T(128)}, u32[]{:S(2)}) copy-start(f32[128]{0:T(128)} %copy-done.50) | copy-start | bytes 1540
  384.0 91.5 %copy-start.53 = (f32[128]{0:T(128)S(1)}, f32[128]{0:T(128)}, u32[]{:S(2)}) copy-start(f32[128]{0:T(128)} %copy-done.52) | copy-start | bytes 1540
  384.0 91.5 %copy-start.55 = (f32[128]{0:T(128)S(1)}, f32[128]{0:T(128)}, u32[]{:S(2)}) copy-start(f32[128]{0:T(128)} %copy-done.54) | copy-start | bytes 1540
  384.0 91.5 %copy-start.57 = (f32[128]{0:T(128)S(1)}, f32[128]{0:T(128)}, u32[]{:S(2)}) copy-start(f32[128]{0:T(128)} %copy-done.56) | copy-start | bytes 1540
  384.1 91.5 %copy-start.59 = (f32[128]{0:T(128)S(1)}, f32[128]{0:T(128)}, u32[]{:S(2)}) copy-start(f32[128]{0:T(128)} %copy-done.58) | copy-start | bytes 1540
  384.1 91.5 %copy-start.61 = (f32[128]{0:T(128)S(1)}, f32[128]{0:T(128)}, u32[]{:S(2)}) copy-start(f32[128]{0:T(128)} %copy-done.60) | copy-start | bytes 1540
  384.1 91.5 %copy-start.63 = (f32[128]{0:T(128)S(1)}, f32[128]{0:T(128)}, u32[]{:S(2)}) copy-start(f32[128]{0:T(128)} %copy-done.62) | copy-start | bytes 1540
  384.1 91.5 %copy-start.65 = (f32[128]{0:T(128)S(1)}, f32[128]{0:T(128)}, u32[]{:S(2)}) copy-start(f32[128]{0:T(128)} %copy-done.64) | copy-start | bytes 1540
  384.1 91.5 %copy-start.67 = (f32[128]{0:T(128)S(1)}, f32[128]{0:T(128)}, u32[]{:S(2)}) copy-start(f32[128]{0:T(128)} %copy-done.66) | copy-start | bytes 1540
  384.1 91.5 %copy-start.69 = (f32[128]{0:T(128)S(1)}, f32[128]{0:T(128)}, u32[]{:S(2)}) copy-start(f32[128]{0:T(128)} %copy-done.68) | copy-start | bytes 1540
  384.1 91.5 %copy-start.71 = (f32[128]{0:T(128)S(1)}, f32[128]{0:T(128)}, u32[]{:S(2)}) copy-start(f32[128]{0:T(128)} %copy-done.70) | copy-start | bytes 1540
  384.1 91.5 %copy-start.73 = (f32[128]{0:T(128)S(1)}, f32[128]{0:T(128)}, u32[]{:S(2)}) copy-start(f32[128]{0:T(128)} %copy-done.72) | copy-start | bytes 1540
  (67 other events, 2743.9 us)
Sparse Core Ops, SparseCore 0:
  17.9 55.9 all-gather.4
  90.0 103.0 reduce-scatter.2
  195.8 84.4 all-gather.8
  302.3 51.3 all-gather.6
  369.4 102.9 reduce-scatter.4
